TPU v7x, 256 devices: a whole 4x4x8 slice. The times are simulated.
256 devices in a mesh: row: 8 (over z_lo, y), col: 4 (over z_hi), depth: 8 (over x, core).
Axes of the slice: x: 4, y: 4, z: 8 (z_hi: 4, z_lo: 2; z = z_hi * 2 + z_lo), core: 2. Of those that a mesh axis runs over, the one named last changes fastest.
Arguments:
- tokens: bfloat16 [2048, 12288], P(('row', 'col'), 'depth'), may hold values from -6 to 6
- weight: bfloat16 [12288, 24576], P('depth', ('row', 'col')), may hold values from -5 to 5
- moment: bfloat16 [12288, 24576], P('depth', ('row', 'col')), may hold values from -0.59765625 to 0.59765625
- upstream: bfloat16 [8, 256, 24576], P(None, 'col', ('row', 'depth')), may hold values from -24 to 24
Outputs:
- activated: bfloat16 [8, 256, 24576], P(None, 'col', ('row', 'depth'))
- new_weight: bfloat16 [12288, 24576], P('depth', ('row', 'col'))
- new_moment: bfloat16 [12288, 24576], P('depth', ('row', 'col'))
All inputs are finite; a program needn't handle non-finite values.
Results may differ from a plain program's by a relative error of at most 0.015.
Values may be sent and summed in bfloat16 or wider, within the bound.
A program may use at most 64 MiB of HBM per device.

v0:
```python
import jax
import jax.numpy as jnp
from jax import lax
from jax.sharding import PartitionSpec as P

D = 12288
gelu_coef = 0.7978845608028654
cubic_coef = 0.044715
lion_rate = 0.5
decay_rate = 0.1
beta_one = 0.9
beta_two = 0.99
smooth_tau = 0.1


def gelu_pair(preact):
    tangent = jnp.tanh(gelu_coef * (preact + cubic_coef * preact * preact * preact))
    gelu_value = 0.5 * preact * (1.0 + tangent)
    gelu_slope = 0.5 * (1.0 + tangent) + 0.5 * preact * (1.0 - tangent * tangent) * gelu_coef * (
        1.0 + 3.0 * cubic_coef * preact * preact
    )
    return (gelu_value, gelu_slope)


def shards(tokens, weight, moment, upstream):
    row_count = lax.axis_size("row")
    tok_rows = tokens.shape[0]
    fan_scale = D ** (-0.5)
    gathered = lax.all_gather(tokens, "row", axis=0, tiled=True)
    partial_value = jnp.dot(
        gathered,
        lax.all_gather(weight, "col", axis=1, tiled=True),
        preferred_element_type=jnp.float32,
    )
    summed = lax.psum_scatter(
        partial_value.astype(jnp.bfloat16), "depth", scatter_dimension=1, tiled=True
    ).astype(jnp.float32)
    gelu_value, gelu_slope = gelu_pair(summed * fan_scale)
    activated = gelu_value.astype(jnp.bfloat16)
    upstream_flat = upstream.reshape(row_count * tok_rows, upstream.shape[2]).astype(jnp.float32)
    local_grad = (upstream_flat * gelu_slope).astype(jnp.bfloat16)
    act_grad = lax.all_gather(local_grad, "depth", axis=1, tiled=True)
    grad_panel = lax.dot_general(
        gathered, act_grad, (((0,), (0,)), ((), ())), preferred_element_type=jnp.float32
    )
    grad_sum = lax.psum_scatter(
        grad_panel.astype(jnp.bfloat16), "col", scatter_dimension=1, tiled=True
    ).astype(jnp.float32)
    grad_full = grad_sum * fan_scale
    moment_f = moment.astype(jnp.float32)
    weight_f = weight.astype(jnp.float32)
    blended = beta_one * moment_f + (1.0 - beta_one) * grad_full
    update = blended / jnp.sqrt(blended * blended + smooth_tau * smooth_tau)
    new_weight = (weight_f - lion_rate * (update + decay_rate * weight_f)).astype(jnp.bfloat16)
    new_moment = (beta_two * moment_f + (1.0 - beta_two) * grad_full).astype(jnp.bfloat16)
    activated = activated.reshape(upstream.shape[0], upstream.shape[1], activated.shape[1])
    return (activated, new_weight, new_moment)


def solution(mesh):
    placed = (
        P(("row", "col"), "depth"),
        P("depth", ("row", "col")),
        P("depth", ("row", "col")),
        P(None, "col", ("row", "depth")),
    )
    return jax.shard_map(
        shards,
        mesh=mesh,
        in_specs=placed,
        out_specs=(
            P(None, "col", ("row", "depth")),
            P("depth", ("row", "col")),
            P("depth", ("row", "col")),
        ),
        check_vma=False,
    )
```

profile of v0, /device:TPU:2, one launch (start us, length us, event | category | flops | bytes accessed | tf_op | source)
XLA Modules:
  0.0 509.9 jit_solution(10022676626198729526)
XLA Ops:
  7.2 0.0 all-gather.4.cloned.1.call-start
  7.2 0.7 all-gather.4.cloned.1.call-update
  7.9 0.0 all-gather.6.cloned.1.call-start
  7.9 0.7 all-gather.6.cloned.1.call-update
  8.6 0.0 reduce-scatter.7.cloned.1.call-start
  8.7 47.2 %all-gather.4.cloned.1.call-done = bf16[512,1536]{1,0:T(8,128)(2,1)} async-done(((bf16[64,1536]{1,0:T(8,128)(2,1)}), bf16[512,1536]{1,0:T(8,128)(2,1)}) %all-gather.4.cloned.1.call-update) | async-done | bytes 1572880 | tf_op jit(solution)/shard_map/all_gather | solution.py:29
  55.9 173.9 %all-gather.6.cloned.1.call-done = bf16[1536,3072]{1,0:T(8,128)(2,1)} async-done(((bf16[1536,768]{1,0:T(8,128)(2,1)}), bf16[1536,3072]{1,0:T(8,128)(2,1)}) %all-gather.6.cloned.1.call-update) | async-done | bytes 9437200 | tf_op jit(solution)/shard_map/all_gather | solution.py:32
  229.8 8.1 %convolution_convert_fusion.1 = bf16[512,3072]{1,0:T(8,128)(2,1)S(1)} fusion(bf16[512,1536]{1,0:T(8,128)(2,1)} %all-gather.4.cloned.1.call-done, bf16[1536,3072]{1,0:T(8,128)(2,1)} %all-gather.6.cloned.1.call-done), kind=kOutput, calls=%fused_computation.14 | convolution fusion | flops 4833411072 | bytes 14155776 | tf_op jit(solution)/shard_map/dot_general | solution.py:30
  237.9 2.8 copy.15
  240.8 0.0 all-gather.8.cloned.1.call-start
  240.8 33.4 %reduce-scatter.7.cloned.1.call-done = bf16[384,512]{1,0:T(8,128)(2,1)} async-done(((bf16[3072,512]{1,0:T(8,128)(2,1)}), bf16[384,512]{1,0:T(8,128)(2,1)}) %reduce-scatter.7.cloned.1.call-update) | async-done | bytes 393232
  274.2 1.2 copy.16
  275.4 1.5 fusion.18
  277.0 0.0 all-gather.8.cloned.1.call-update
  277.0 0.0 reduce-scatter.5.cloned.1.call-start
  277.0 31.8 %all-gather.8.cloned.1.call-done = bf16[512,3072]{1,0:T(8,128)(2,1)} async-done(((bf16[512,384]{1,0:T(8,128)(2,1)}), bf16[512,3072]{1,0:T(8,128)(2,1)}) %all-gather.8.cloned.1.call-update) | async-done | bytes 3145744 | tf_op jit(solution)/shard_map/all_gather | solution.py:42
  308.8 9.6 %fusion = bf16[1536,3072]{0,1:T(8,128)(2,1)} fusion(bf16[512,3072]{1,0:T(8,128)(2,1)} %all-gather.8.cloned.1.call-done, bf16[512,1536]{1,0:T(8,128)(2,1)S(1)} %copy-done.4), kind=kOutput, calls=%fused_computation.1 | convolution fusion | flops 4836556800 | bytes 14155776 | tf_op jit(solution)/shard_map/dot_general | solution.py:43
  318.4 1.6 copy-done
  320.1 2.4 copy.11
  322.5 4.4 copy.12
  326.9 163.8 %reduce-scatter.5.cloned.1.call-done = bf16[1536,768]{0,1:T(8,128)(2,1)} async-done(((bf16[1536,3072]{0,1:T(8,128)(2,1)}), bf16[1536,768]{0,1:T(8,128)(2,1)}) %reduce-scatter.5.cloned.1.call-update) | async-done | bytes 2359312 | tf_op jit(solution)/shard_map/reduce_scatter | solution.py:46
  490.7 5.9 %fusion.6 = (bf16[1536,768]{0,1:T(8,128)(2,1)}, bf16[1536,768]{0,1:T(8,128)(2,1)}) fusion(bf16[1536,768]{0,1:T(8,128)(2,1)} %copy.12, bf16[1536,768]{0,1:T(8,128)(2,1)} %reduce-scatter.5.cloned.1.call-done, bf16[1536,768]{0,1:T(8,128)(2,1)S(1)} %copy-done.1), kind=kLoop, calls=%fused_computation.13 | loop fusion | flops 21233664 | bytes 11796480 | tf_op jit(solution)/shard_map/convert_element_type | solution.py:55
  496.6 4.4 copy.13
  501.0 2.4 copy.14
  (11 shorter events, 0.1 us)
Async XLA Ops:
  7.2 48.8 %all-gather.4.cloned.1.call-start = ((), (), s32[]{:S(2)}) async-start(), calls=%async_computation.2 | async-start | bytes 1769472 | tf_op jit(solution)/shard_map/all_gather | solution.py:29
  7.9 221.9 %all-gather.6.cloned.1.call-start = ((), (), s32[]{:S(2)}) async-start(), calls=%async_computation.3 | async-start | bytes 11796480 | tf_op jit(solution)/shard_map/all_gather | solution.py:32
  8.6 265.6 %reduce-scatter.7.cloned.1.call-start = ((), (), s32[]{:S(2)}) async-start(), calls=%async_computation.6 | async-start | bytes 3538944
  237.9 37.5 %copy-start.3 = (bf16[8,64,384]{2,1,0:T(8,128)(2,1)S(1)}, bf16[8,64,384]{2,1,0:T(8,128)(2,1)}, u32[]{:S(2)}) copy-start(bf16[8,64,384]{2,1,0:T(8,128)(2,1)} %param.7) | copy-start | bytes 1179652
  240.7 68.1 %copy-start.4 = (bf16[512,1536]{1,0:T(8,128)(2,1)S(1)}, bf16[512,1536]{1,0:T(8,128)(2,1)}, u32[]{:S(2)}) copy-start(bf16[512,1536]{1,0:T(8,128)(2,1)} %all-gather.4.cloned.1.call-done) | copy-start | bytes 4718596
  240.8 68.0 %all-gather.8.cloned.1.call-start = ((), (), s32[]{:S(2)}) async-start(), calls=%async_computation.4 | async-start | bytes 3538944 | tf_op jit(solution)/shard_map/all_gather | solution.py:42
  277.0 213.7 %reduce-scatter.5.cloned.1.call-start = ((), (), s32[]{:S(2)}) async-start(), calls=%async_computation.5 | async-start | bytes 11796480 | tf_op jit(solution)/shard_map/reduce_scatter | solution.py:46
  318.4 1.7 copy-start
  322.5 168.2 %copy-start.1 = (bf16[1536,768]{0,1:T(8,128)(2,1)S(1)}, bf16[1536,768]{0,1:T(8,128)(2,1)}, u32[]{:S(2)}) copy-start(bf16[1536,768]{0,1:T(8,128)(2,1)} %copy.11) | copy-start | bytes 7077892
  496.6 4.4 copy-start.2
Sparse Core Ops, SparseCore 0:
  9.8 46.0 all-gather.3
  57.7 172.0 all-gather.5
  240.9 33.2 reduce-scatter.6
  277.1 31.6 all-gather.7
  318.5 172.1 reduce-scatter.4
where the time goes:
time: 510 us
  waiting for transfers between devices  452 us (89%)
  local copies, waits for them, and re-layouts  19.4 us (4%)
  matrix products  17.7 us (3%)
  between operations  13.8 us (3%)
  other arithmetic  7.4 us (1%)
    all_gather x1, waiting for transfers between devices, shards(): lax.all_gather(weight, 'col', axis=1, tiled=True)  174 us
    reduce_scatter x1, waiting for transfers between devices, shards(): lax.psum_scatter(grad_panel.astype(jnp.bfloat16), 'col', scatter_dimensio...  164 us
    all_gather x1, waiting for transfers between devices, shards(): gathered = lax.all_gather(tokens, 'row', axis=0, tiled=True)  47.2 us
    unnamed x6, waiting for transfers between devices  34.8 us
    all_gather x1, waiting for transfers between devices, shards(): act_grad = lax.all_gather(local_grad, 'depth', axis=1, tiled=True)  31.8 us
    unnamed x16, local copies, waits for them, and re-layouts  19.4 us
  transfers between devices with their start and end apart: 5, of which 5 were waited for; matrix products, arithmetic and copies ran while one was open for 1% of the time, Pallas kernels for 0%

commit v1 on v0

--- a/solution.py
+++ b/solution.py
@@ -1,3 +1,4 @@
+import functools
 import jax
 import jax.numpy as jnp
 from jax import lax
@@ -11,6 +12,16 @@
 beta_one = 0.9
 beta_two = 0.99
 smooth_tau = 0.1
+
+
+def proceed_field(x0, peer_axis):
+    parts_out = jnp.concatenate(
+        lax.all_to_all(jnp.stack([x0 for _ in range(lax.psum(1, peer_axis))]), peer_axis, 0, 0), 1
+    )
+    return parts_out
+
+
+produce_circles_on_mesh = functools.partial(proceed_field, peer_axis="col")
 
 
 def gelu_pair(preact):
@@ -28,9 +39,7 @@
     fan_scale = D ** (-0.5)
     gathered = lax.all_gather(tokens, "row", axis=0, tiled=True)
     partial_value = jnp.dot(
-        gathered,
-        lax.all_gather(weight, "col", axis=1, tiled=True),
-        preferred_element_type=jnp.float32,
+        gathered, produce_circles_on_mesh(weight), preferred_element_type=jnp.float32
     )
     summed = lax.psum_scatter(
         partial_value.astype(jnp.bfloat16), "depth", scatter_dimension=1, tiled=True

time: 510 us -> 527 us (1.033)
  starting transfers between devices: 0.2 us -> 8.58 us
    all_gather x1 -> x0, waiting for transfers between devices: 174 us -> none  [shards(): lax.all_gather(weight, 'col', axis=1, tiled=True)]
    all_to_all x0 -> x1, waiting for transfers between devices: none -> 125 us  [proceed_field(): lax.all_to_all(jnp.stack([x0 for _ in range(lax.psum(1, peer_axis))]), pe...]
    all_gather x1, waiting for transfers between devices: 47.2 us -> 96.9 us  [shards(): gathered = lax.all_gather(tokens, 'row', axis=0, tiled=True)]
    all_to_all x0 -> x1, starting transfers between devices: none -> 8.46 us  [proceed_field(): lax.all_to_all(jnp.stack([x0 for _ in range(lax.psum(1, peer_axis))]), pe...]
    unnamed x6 -> x5, waiting for transfers between devices: 34.8 us -> 32.4 us
    unnamed x16 -> x10, local copies, waits for them, and re-layouts: 19.4 us -> 19.9 us
where the time goes in v1:
time: 527 us; the launch traced here: 525 us
  waiting for transfers between devices  453 us (86%)
  local copies, waits for them, and re-layouts  24.3 us (5%)
  matrix products  18.7 us (4%)
  between operations  13.8 us (3%)
  starting transfers between devices  8.58 us (2%)
  other arithmetic  7.39 us (1%)
    reduce_scatter x1, waiting for transfers between devices, shards(): lax.psum_scatter(grad_panel.astype(jnp.bfloat16), 'col', scatter_dimensio...  166 us
    all_to_all x1, waiting for transfers between devices, proceed_field(): lax.all_to_all(jnp.stack([x0 for _ in range(lax.psum(1, peer_axis))]), pe...  125 us
    all_gather x1, waiting for transfers between devices, shards(): gathered = lax.all_gather(tokens, 'row', axis=0, tiled=True)  96.9 us
    unnamed x5, waiting for transfers between devices  32.4 us
    all_gather x1, waiting for transfers between devices, shards(): act_grad = lax.all_gather(local_grad, 'depth', axis=1, tiled=True)  31.7 us
    unnamed x10, local copies, waits for them, and re-layouts  19.9 us
  transfers between devices with their start and end apart: 5, of which 5 were waited for; matrix products, arithmetic and copies ran while one was open for 1% of the time, Pallas kernels for 0%

profile of v1, /device:TPU:2, one launch (start us, length us, event | category | flops | bytes accessed | tf_op | source)
XLA Modules:
  0.0 525.2 jit_solution(7104985426650204329)
XLA Ops:
  7.2 2.8 copy.16
  10.0 4.4 stack.2
  14.4 8.5 %all-to-all-start = ((bf16[4,1536,768]{1,2,0:T(8,128)(2,1)}), bf16[4,1536,768]{1,2,0:T(8,128)(2,1)}, u32[]{:S(2)}, u32[]{:S(2)}) async-start(bf16[4,1536,768]{1,2,0:T(8,128)(2,1)} %stack.2), calls=%async_computation | async-start | bytes 18874368 | tf_op jit(solution)/shard_map/all_to_all | solution.py:19
  22.9 0.7 all-gather.3.cloned.1.call-update
  23.6 0.0 reduce-scatter.7.cloned.1.call-start
  23.6 96.9 %all-gather.3.cloned.1.call-done = bf16[512,1536]{1,0:T(8,128)(2,1)} async-done(((bf16[64,1536]{1,0:T(8,128)(2,1)}), bf16[512,1536]{1,0:T(8,128)(2,1)}) %all-gather.3.cloned.1.call-update) | async-done | bytes 1572880 | tf_op jit(solution)/shard_map/all_gather | solution.py:40
  120.5 125.3 %all-to-all-done = bf16[4,1536,768]{1,2,0:T(8,128)(2,1)} async-done(((bf16[4,1536,768]{1,2,0:T(8,128)(2,1)}), bf16[4,1536,768]{1,2,0:T(8,128)(2,1)}, u32[]{:S(2)}, u32[]{:S(2)}) %all-to-all-start) | async-done | bytes 9437216 | tf_op jit(solution)/shard_map/all_to_all | solution.py:19
  245.8 9.3 %convolution_convert_fusion.1 = bf16[512,3072]{1,0:T(8,128)(2,1)} fusion(bf16[512,1536]{1,0:T(8,128)(2,1)} %all-gather.3.cloned.1.call-done, bf16[1536,3072]{0,1:T(8,128)(2,1)} %bitcast.1), kind=kOutput, calls=%fused_computation.14 | convolution fusion | flops 4833411072 | bytes 14155776 | tf_op jit(solution)/shard_map/dot_general | solution.py:41
  255.1 4.7 copy.21
  259.8 0.0 reduce-scatter.7.cloned.1.call-update
  259.8 0.0 all-gather.5.cloned.1.call-start
  259.9 31.7 %reduce-scatter.7.cloned.1.call-done = bf16[384,512]{1,0:T(8,128)(2,1)} async-done(((bf16[3072,512]{1,0:T(8,128)(2,1)}), bf16[384,512]{1,0:T(8,128)(2,1)}) %reduce-scatter.7.cloned.1.call-update) | async-done | bytes 393232
  291.5 1.2 copy.22
  292.7 1.5 fusion.18
  294.3 0.0 all-gather.5.cloned.1.call-update
  294.3 0.0 reduce-scatter.5.cloned.1.call-start
  294.4 31.7 %all-gather.5.cloned.1.call-done = bf16[512,3072]{1,0:T(8,128)(2,1)} async-done(((bf16[512,384]{1,0:T(8,128)(2,1)}), bf16[512,3072]{1,0:T(8,128)(2,1)}) %all-gather.5.cloned.1.call-update) | async-done | bytes 3145744 | tf_op jit(solution)/shard_map/all_gather | solution.py:51
  326.1 9.4 %fusion = bf16[1536,3072]{0,1:T(8,128)(2,1)} fusion(bf16[512,3072]{1,0:T(8,128)(2,1)} %all-gather.5.cloned.1.call-done, bf16[512,1536]{1,0:T(8,128)(2,1)} %all-gather.3.cloned.1.call-done), kind=kOutput, calls=%fused_computation.1 | convolution fusion | flops 4836556800 | bytes 14155776 | tf_op jit(solution)/shard_map/dot_general | solution.py:52
  335.5 0.0 reduce-scatter.5.cloned.1.call-update
  335.5 4.3 copy.18
  339.8 166.2 %reduce-scatter.5.cloned.1.call-done = bf16[1536,768]{0,1:T(8,128)(2,1)} async-done(((bf16[1536,3072]{0,1:T(8,128)(2,1)}), bf16[1536,768]{0,1:T(8,128)(2,1)}) %reduce-scatter.5.cloned.1.call-update) | async-done | bytes 2359312 | tf_op jit(solution)/shard_map/reduce_scatter | solution.py:55
  506.0 5.9 %fusion.6 = (bf16[1536,768]{0,1:T(8,128)(2,1)}, bf16[1536,768]{0,1:T(8,128)(2,1)}) fusion(bf16[1536,768]{0,1:T(8,128)(2,1)} %copy.18, bf16[1536,768]{0,1:T(8,128)(2,1)} %reduce-scatter.5.cloned.1.call-done, bf16[1536,768]{0,1:T(8,128)(2,1)S(1)} %copy.16), kind=kLoop, calls=%fused_computation.13 | loop fusion | flops 21233664 | bytes 11796480 | tf_op jit(solution)/shard_map/convert_element_type | solution.py:64
  511.9 4.4 copy.19
  516.3 2.4 copy.20
  (5 shorter events, 0.0 us)
Async XLA Ops:
  14.4 231.4 %all-to-all-start = ((bf16[4,1536,768]{1,2,0:T(8,128)(2,1)}), bf16[4,1536,768]{1,2,0:T(8,128)(2,1)}, u32[]{:S(2)}, u32[]{:S(2)}) async-start(bf16[4,1536,768]{1,2,0:T(8,128)(2,1)} %stack.2), calls=%async_computation | async-start | bytes 18874368 | tf_op jit(solution)/shard_map/all_to_all | solution.py:19
  22.8 97.7 %all-gather.3.cloned.1.call-start = ((), (), s32[]{:S(2)}) async-start(), calls=%async_computation.3 | async-start | bytes 1769472 | tf_op jit(solution)/shard_map/all_gather | solution.py:40
  23.6 268.0 %reduce-scatter.7.cloned.1.call-start = ((), (), s32[]{:S(2)}) async-start(), calls=%async_computation.6 | async-start | bytes 3538944
  255.1 37.6 %copy-start.1 = (bf16[8,64,384]{2,1,0:T(8,128)(2,1)S(1)}, bf16[8,64,384]{2,1,0:T(8,128)(2,1)}, u32[]{:S(2)}) copy-start(bf16[8,64,384]{2,1,0:T(8,128)(2,1)} %param.7) | copy-start | bytes 1179652
  259.8 66.3 %all-gather.5.cloned.1.call-start = ((), (), s32[]{:S(2)}) async-start(), calls=%async_computation.4 | async-start | bytes 3538944 | tf_op jit(solution)/shard_map/all_gather | solution.py:51
  294.3 211.7 %reduce-scatter.5.cloned.1.call-start = ((), (), s32[]{:S(2)}) async-start(), calls=%async_computation.5 | async-start | bytes 11796480 | tf_op jit(solution)/shard_map/reduce_scatter | solution.py:55
  511.9 4.4 copy-start
Sparse Core Ops, SparseCore 0:
  25.5 95.0 all-gather.2
  259.9 31.5 reduce-scatter.6
  294.4 31.6 all-gather.4
  335.6 170.3 reduce-scatter.4
